TPU v7x, 128 devices: a whole 4x4x4 slice. The times are simulated.
128 devices in a mesh: lat: 16 (over x, y), lon: 8 (over z, core).
Axes of the slice: x: 4, y: 4, z: 4, core: 2. Of those that a mesh axis runs over, the one named last changes fastest.
Arguments:
- cotangent: bfloat16 [16384, 16, 128], P(('lat', 'lon')), may hold values from -6 to 6
- fractions: float32 [16384, 2, 128], P(('lat', 'lon')), may hold values from 0 to 1
- offsets: int32 [16384, 2, 128], P(('lat', 'lon')), may hold values from 0 to 7
- owner: int32 [16384, 1], P(('lat', 'lon')), may hold values from 0 to 127; in each aligned block of 128 rows (0 to 127, 128 to 255, ...) at most 2 rows name the same one
- sub_block: int32 [16384], P(('lat', 'lon')), may hold values from 0 to 255
- lon_inverse: float32 [2048, 2048], replicated, may hold values from -0.125 to 0.125
- lat_inverse: float32 [1024, 1024], replicated, may hold values from -0.1875 to 0.1875
Outputs:
- tracer_adjoint: float32 [16, 1024, 2048], P('lon', None, 'lat')
Inputs may be any that keep to these rules, and one draw needn't show every extreme that they name: Among the 128 arrival blocks of one device no owner is named more than 2 times; some owner is named exactly 2 times.
All inputs are finite; a program needn't handle non-finite values.
Results may differ from a plain program's by a relative error of at most 0.0029.
The roundings to bfloat16 on the way count: a program that leaves them out, or rounds other values in their place, can miss the bound.
Values may be sent and summed in bfloat16 or wider, within the bound.
A program may use at most 128 MiB of HBM per device.

v0:
```python
import jax
import jax.numpy as jnp
from jax import lax
from jax.sharding import PartitionSpec as P

BS = 8
CLAT = 64
CLON = 256


def with_halo(block, sides, width, periodic):
    for axis, dim in sides:
        count = lax.axis_size(axis)
        forward = [(i, i + 1) for i in range(count - 1)]
        if periodic:
            forward.append((count - 1, 0))
        backward = [(target, source) for source, target in forward]
        low = lax.ppermute(
            lax.slice_in_dim(block, block.shape[dim] - width, None, axis=dim), axis, forward
        )
        high = lax.ppermute(lax.slice_in_dim(block, 0, width, axis=dim), axis, backward)
        block = jnp.concatenate([low, block, high], axis=dim)
    return block


def spline_weights(t):
    cube = t * t * t
    square = t * t
    return jnp.stack(
        [
            (1.0 - t) ** 3 / 6.0,
            (3.0 * cube - 6.0 * square + 4.0) / 6.0,
            (-3.0 * cube + 3.0 * square + 3.0 * t + 1.0) / 6.0,
            cube / 6.0,
        ]
    )


def window_table(frac, offset):
    weights = spline_weights(frac)
    places = jnp.arange(2 * BS, dtype=jnp.int32)
    table = jnp.zeros((frac.shape[0], 2 * BS, frac.shape[1]), jnp.float32)
    for step in range(4):
        match = offset[:, None, :] + step == places[None, :, None]
        table = table + jnp.where(match, weights[step][:, None, :], 0.0)
    return table


def build_window(grads, frac, offset):
    count = grads.shape[0]
    lat_table = window_table(frac[:, 0], offset[:, 0])
    lon_table = window_table(frac[:, 1], offset[:, 1])
    stencil = (
        (lat_table[:, :, None, :] * lon_table[:, None, :, :])
        .reshape(count, 4 * BS * BS, grads.shape[2])
        .astype(jnp.bfloat16)
    )
    return lax.dot_general(
        grads, stencil, (((2,), (2,)), ((0,), (0,))), preferred_element_type=jnp.float32
    ).astype(jnp.bfloat16)


def fold_halves(blocks, block_axis, half_axis):
    first = jnp.take(blocks, 0, axis=half_axis)
    second = jnp.take(blocks, 1, axis=half_axis)
    pad_after = [(0, 0)] * first.ndim
    pad_before = [(0, 0)] * first.ndim
    pad_after[block_axis] = (0, 1)
    pad_before[block_axis] = (1, 0)
    return jnp.pad(first, pad_after) + jnp.pad(second, pad_before)


def on_device(cotangent, fractions, offsets, owner, sub_block, lon_inverse, lat_inverse):
    count, chans, points = cotangent.shape
    lat_count = lax.axis_size("lat")
    lon_count = lax.axis_size("lon")
    devices = lat_count * lon_count
    slots = max(2, 2 * count // devices)
    total = devices * slots
    span = 2 * BS
    down = CLAT // BS
    across = CLON // BS
    target = owner[:, 0]
    order = jnp.arange(count, dtype=jnp.int32)
    earlier = (target[None, :] == target[:, None]) & (order[None, :] < order[:, None])
    place = target * slots + jnp.sum(earlier.astype(jnp.int32), axis=1)
    select = place[None, :] == jnp.arange(total, dtype=jnp.int32)[:, None]
    labels = jnp.max(jnp.where(select, sub_block[None, :], -1), axis=1)
    flat_shape = (devices, slots)
    window = build_window(cotangent, fractions, offsets)
    packed = jnp.dot(
        select.astype(jnp.bfloat16),
        window.reshape(count, chans * span * span),
        preferred_element_type=jnp.float32,
    ).astype(jnp.bfloat16)
    got, got_labels = (
        lax.all_to_all(
            packed.reshape(flat_shape + (chans * span * span,)),
            ("lat", "lon"),
            split_axis=0,
            concat_axis=0,
            tiled=True,
        ),
        lax.all_to_all(
            labels.reshape(flat_shape), ("lat", "lon"), split_axis=0, concat_axis=0, tiled=True
        ),
    )
    got = got.reshape(total, chans * span * span)
    got_labels = got_labels.reshape(total)
    gather_sel = got_labels[None, :] == jnp.arange(down * across, dtype=jnp.int32)[:, None]
    summed = jnp.dot(gather_sel.astype(jnp.bfloat16), got, preferred_element_type=jnp.float32)
    summed = summed.reshape(down, across, chans, 2, BS, 2, BS)
    rows_done = fold_halves(summed, 0, 3)
    cols_done = fold_halves(rows_done, 1, 4)
    extended = jnp.transpose(cols_done, (2, 0, 3, 1, 4)).reshape(
        chans, (down + 1) * BS, (across + 1) * BS
    )
    width = extended.shape[2]
    blank_row = jnp.zeros((chans, 1, width), jnp.float32)
    lat_rim = jnp.concatenate(
        [extended[:, 0:1], blank_row, extended[:, CLAT + 1 : CLAT + 3]], axis=1
    )
    lat_got = with_halo(lat_rim.astype(jnp.bfloat16), (("lat", 1),), 2, False).astype(lat_rim.dtype)
    core = extended[:, 1 : CLAT + 1]
    core = core.at[:, 0:2].add(lat_got[:, 0:2])
    core = core.at[:, CLAT - 1 : CLAT].add(lat_got[:, 6:7])
    blank_col = jnp.zeros((chans, CLAT, 1), jnp.float32)
    lon_rim = jnp.concatenate([core[:, :, 0:1], blank_col, core[:, :, CLON + 1 : CLON + 3]], axis=2)
    lon_got = with_halo(lon_rim, (("lon", 2),), 2, True)
    tile = core[:, :, 1 : CLON + 1]
    tile = tile.at[:, :, 0:2].add(lon_got[:, :, 0:2])
    tile = tile.at[:, :, CLON - 1 : CLON].add(lon_got[:, :, 6:7])
    lines = lax.all_to_all(tile, "lon", split_axis=0, concat_axis=2, tiled=True)
    share = lines.shape[0]
    lon_adjoint = jnp.dot(
        lines.reshape(share * CLAT, lines.shape[2]), lon_inverse, precision=lax.Precision.HIGHEST
    ).reshape(share, CLAT, lines.shape[2])
    columns = lax.all_to_all(lon_adjoint, "lat", split_axis=2, concat_axis=1, tiled=True)
    return lax.dot_general(
        lat_inverse, columns, (((0,), (1,)), ((), ())), precision=lax.Precision.HIGHEST
    ).transpose(1, 0, 2)


def solution(mesh):
    return jax.shard_map(
        on_device,
        mesh=mesh,
        in_specs=(
            P(("lat", "lon"), None, None),
            P(("lat", "lon"), None, None),
            P(("lat", "lon"), None, None),
            P(("lat", "lon"), None),
            P(("lat", "lon")),
            P(),
            P(),
        ),
        out_specs=P("lon", None, "lat"),
        check_vma=False,
    )
```

profile of v0, /device:TPU:1, one launch (start us, length us, event | category | flops | bytes accessed | tf_op | source)
XLA Modules:
  0.0 220.4 jit_solution(13024532161906242834)
XLA Ops:
  0.0 0.9 convert_reduce_fusion
  1.6 0.8 select_reduce_fusion
  2.3 0.8 all_to_all.33
  3.1 11.5 %all-to-all-start = ((s32[128,1,2]{2,1,0:T(1,128)}), s32[128,1,2]{2,1,0:T(1,128)S(1)}, u32[]{:S(2)}, u32[]{:S(2)}) async-start(s32[128,1,2]{2,1,0:T(1,128)} %bitcast.1), calls=%async_computation | async-start | bytes 131072 | tf_op jit(solution)/shard_map/all_to_all | solution.py:104
  14.6 1.3 fusion.24
  15.9 1.7 fusion.19
  17.6 2.4 %select_add_fusion = (f32[128,16,128]{2,1,0:T(8,128)}, f32[128,16,128]{2,1,0:T(8,128)}) fusion(f32[128,128]{1,0:T(8,128)S(1)} %bitcast.101, s32[128,128]{1,0:T(8,128)S(1)} %bitcast.94, f32[128,128]{1,0:T(8,128)S(1)} %bitcast.102, s32[128,128]{1,0:T(8,128)S(1)} %bitcast.93, f32[128,128]{1,0:T(8,128)S(1)} %bitcast.100, s32[128,128]{1,0:T(8,128)S(1)} %bitcast.92, ...), kind=kLoop, calls=%fused_computation.20 | loop fusion | flops 5767168 | bytes 3145728 | tf_op jit(solution)/shard_map/add | solution.py:45
  20.0 4.2 %multiply_convert_fusion = bf16[128,16,16,128]{3,2,1,0:T(8,128)(2,1)S(1)} fusion(f32[128,16,128]{2,1,0:T(8,128)} %get-tuple-element.125, f32[128,16,128]{2,1,0:T(8,128)} %get-tuple-element.126), kind=kLoop, calls=%fused_computation.2 | loop fusion | flops 8388608 | bytes 10485760 | tf_op jit(solution)/shard_map/convert_element_type | solution.py:56
  24.2 2.3 %convolution_convert_fusion.1 = bf16[128,256,16]{1,2,0:T(8,128)(2,1)S(1)} fusion(bf16[128,256,128]{2,1,0:T(8,128)(2,1)S(1)} %bitcast.78, bf16[128,16,128]{2,1,0:T(8,128)(2,1)S(1)} %copy-done), kind=kOutput, calls=%fused_computation.18 | convolution fusion | flops 134742016 | bytes 9961472 | tf_op jit(solution)/shard_map/dot_general | solution.py:58
  26.9 0.7 convolution_convert_fusion
  27.6 2.6 %reshape.218 = bf16[128,2,4096]{2,1,0:T(2,128)(2,1)} reshape(bf16[256,4096]{1,0:T(8,128)(2,1)S(1)} %convolution_convert_fusion) | data formatting | bytes 4194304 | tf_op jit(solution)/shard_map/reshape | solution.py:98
  30.3 9.8 %all-to-all-start.1 = ((bf16[128,2,4096]{2,1,0:T(2,128)(2,1)}), bf16[128,2,4096]{2,1,0:T(2,128)(2,1)S(1)}, u32[]{:S(2)}, u32[]{:S(2)}) async-start(bf16[128,2,4096]{2,1,0:T(2,128)(2,1)} %reshape.218), calls=%async_computation.1 | async-start | bytes 4194304 | tf_op jit(solution)/shard_map/all_to_all | solution.py:97
  40.6 0.8 reduce.11
  41.5 29.0 %all-to-all-done.1 = bf16[128,2,4096]{2,1,0:T(2,128)(2,1)S(1)} async-done(((bf16[128,2,4096]{2,1,0:T(2,128)(2,1)}), bf16[128,2,4096]{2,1,0:T(2,128)(2,1)S(1)}, u32[]{:S(2)}, u32[]{:S(2)}) %all-to-all-start.1) | async-done | bytes 2097184 | tf_op jit(solution)/shard_map/all_to_all | solution.py:97
  70.5 2.2 %reshape.219 = bf16[256,4096]{1,0:T(8,128)(2,1)} reshape(bf16[128,2,4096]{2,1,0:T(2,128)(2,1)S(1)} %all-to-all-done.1) | data formatting | bytes 4194304 | tf_op jit(solution)/shard_map/reshape | solution.py:108
  72.8 3.3 %copy.67 = bf16[4096,256]{1,0:T(8,128)(2,1)S(1)} copy(bf16[4096,256]{0,1:T(8,128)(2,1)} %bitcast.82) | data formatting | bytes 4194304 | tf_op jit(solution)/shard_map/dot_general | solution.py:111
  76.0 2.8 %fusion.7 = f32[8,32,16,2,8,2,8]{1,2,6,5,4,3,0:T(8,128)S(1)} fusion(bf16[16,2,8,2,8,256]{5,4,3,2,1,0:T(8,128)(2,1)S(1)} %bitcast.79, s32[8,32]{1,0:T(8,128)S(1)} %multiply_add_fusion, s32[256]{0:T(256)S(1)} %eq.210), kind=kOutput, calls=%fused_computation.15 | convolution fusion | flops 536936448 | bytes 6293504 | tf_op jit(solution)/shard_map/dot_general | solution.py:111
  78.9 6.3 %slice_bitcast_fusion.1 = (f32[8,32,16,8,2,8]{1,2,5,4,3,0:T(8,128)}, f32[8,32,16,8,2,8]{1,2,5,4,3,0:T(8,128)}) fusion(f32[8,32,16,2,8,2,8]{1,2,6,5,4,3,0:T(8,128)S(1)} %fusion.7), kind=kLoop, calls=%fused_computation.6 | loop fusion | bytes 8388608 | tf_op jit(solution)/shard_map/jit(_take)/gather | solution.py:64
  85.2 6.8 %fusion.3 = (f32[9,32,16,8,8]{1,2,4,3,0:T(8,128)S(1)}, f32[9,32,16,8,8]{1,2,4,3,0:T(8,128)S(1)}) fusion(f32[8,32,16,8,2,8]{1,2,5,4,3,0:T(8,128)} %get-tuple-element.103, f32[8,32,16,8,2,8]{1,2,5,4,3,0:T(8,128)} %get-tuple-element.104), kind=kLoop, calls=%fused_computation.9 | loop fusion | flops 589824 | bytes 6553600 | tf_op jit(solution)/shard_map/jit(_take)/gather | solution.py:64
  92.0 3.5 %add_bitcast_fusion = f32[16,9,8,33,8]{3,0,4,2,1:T(8,128)} fusion(f32[9,32,16,8,8]{1,2,4,3,0:T(8,128)S(1)} %get-tuple-element.102, f32[9,32,16,8,8]{1,2,4,3,0:T(8,128)S(1)} %get-tuple-element.101), kind=kLoop, calls=%fused_computation.12 | loop fusion | flops 304128 | bytes 3575808 | tf_op jit(solution)/shard_map/transpose | solution.py:115
  95.5 8.9 %copy.71 = f32[16,9,8,33,8]{0,4,3,2,1:T(8,128)} copy(f32[16,9,8,33,8]{3,0,4,2,1:T(8,128)} %add_bitcast_fusion) | data formatting | bytes 2433024 | tf_op jit(solution)/shard_map/transpose | solution.py:115
  104.4 4.5 %convert.8 = bf16[16,72,264]{0,2,1:T(8,128)(2,1)S(1)} convert(f32[16,72,264]{0,2,1:T(8,128)} %bitcast.75) | non-fusion elementwise | flops 304128 | bytes 1824768 | tf_op jit(solution)/shard_map/convert.3
  108.9 2.2 collective-permute-start
  111.1 2.0 collective-permute-done
  113.2 1.3 collective-permute-start.1
  114.5 3.9 %slice.240 = f32[16,64,264]{0,2,1:T(8,128)} slice(f32[16,72,264]{0,2,1:T(8,128)S(1)} %bitcast.76), slice={[0:16], [1:65], [0:264]} | slice | bytes 2162688 | tf_op jit(solution)/shard_map/slice | solution.py:124
  118.4 1.0 collective-permute-done.1
  119.5 0.7 fusion.13
  120.2 1.6 fusion.16
  121.8 1.1 slice_select_fusion.1
  122.9 2.4 %collective-permute-start.2 = (f32[16,64,2]{0,2,1:T(2,128)S(1)}, f32[16,64,2]{0,2,1:T(2,128)S(1)}, u32[]{:S(2)}, u32[]{:S(2)}) collective-permute-start(f32[16,64,2]{0,2,1:T(2,128)S(1)} %get-tuple-element.106), channel_id=1, source_target_pairs={{0,1},{1,2},{2,3},{3,4},{4,5},{5,6},{6,7},{7,0},{8,9},{9,10},{10,1... | collective-permute-start | bytes 24584 | tf_op jit(solution)/shard_map/ppermute | solution.py:18
  125.3 4.7 %slice.248 = f32[16,64,256]{0,2,1:T(8,128)S(1)} slice(f32[16,64,264]{0,2,1:T(8,128)} %fusion.16), slice={[0:16], [0:64], [1:257]} | slice | bytes 2097152 | tf_op jit(solution)/shard_map/slice | solution.py:130
  130.0 1.0 collective-permute-start.3
  131.0 1.0 fusion.21
  132.0 1.6 collective-permute-done.3
  133.7 1.6 copy-done.3
  135.3 1.8 scatter-add.19
  137.1 5.3 %copy.72 = f32[16,64,256]{2,1,0:T(8,128)S(1)} copy(f32[16,64,256]{0,2,1:T(8,128)} %scatter-add.19) | data formatting | bytes 2097152 | tf_op jit(solution)/shard_map/scatter-add | solution.py:132
  142.4 20.4 %all_to_all.47 = f32[16,64,256]{2,1,0:T(8,128)S(1)} all-to-all(f32[16,64,256]{2,1,0:T(8,128)S(1)} %copy.72), channel_id=1, replica_groups=mesh['lat'=16,'lon'=8] {'lon'}, dimensions={0} | all-to-all | bytes 2097152 | tf_op jit(solution)/shard_map/all_to_all | solution.py:133
  162.9 12.5 %fusion = f32[2,64,2048]{2,1,0:T(8,128)} fusion(f32[2,64,2048]{2,1,0:T(8,128)S(1)} %bitcast.83, f32[2048,2048]{1,0:T(8,128)} %param.28), kind=kOutput, calls=%fused_computation | convolution fusion | flops 6442450944 | bytes 18874368 | tf_op jit(solution)/shard_map/dot_general | solution.py:135
  175.4 2.7 %copy.74 = f32[2,64,2048]{1,0,2:T(2,128)S(1)} copy(f32[2,64,2048]{2,1,0:T(8,128)} %fusion) | data formatting | bytes 2097152 | tf_op jit(solution)/shard_map/dot_general | solution.py:135
  178.1 3.2 %reshape.358 = f32[16,1,16384]{2,1,0:T(1,128)} reshape(f32[2048,2,64]{2,1,0:T(2,128)S(1)} %bitcast.80) | data formatting | bytes 2097152
  181.3 22.1 %all_to_all.48 = f32[16,1,16384]{2,1,0:T(1,128)S(1)} all-to-all(f32[16,1,16384]{2,1,0:T(1,128)} %reshape.358), channel_id=1, replica_groups=mesh['lat'=16,'lon'=8] {'lat'}, dimensions={0} | all-to-all | bytes 2097152 | tf_op jit(solution)/shard_map/all_to_all | solution.py:138
  204.0 4.4 %reduce.12 = f32[16,16384]{1,0:T(8,128)} reduce(f32[16,1,16384]{2,1,0:T(1,128)S(1)} %all_to_all.48, f32[]{:T(128)} %broadcast.416), dimensions={1}, to_apply=%all_to_all.39.reduce_sub_computation | reduce | bytes 2097156 | tf_op jit(solution)/shard_map/all_to_all | solution.py:138
  208.4 2.7 %reshape.359 = f32[2048,2,64]{2,1,0:T(2,128)S(1)} reshape(f32[16,16384]{1,0:T(8,128)} %reduce.12) | data formatting | bytes 2097152
  211.1 2.1 copy.82
  213.2 5.8 %fusion.10 = f32[2,1024,128]{1,2,0:T(8,128)S(1)} fusion(f32[2,1024,128]{2,1,0:T(8,128)} %bitcast.87, f32[1024,1024]{1,0:T(8,128)} %param.29), kind=kOutput, calls=%fused_computation.19 | convolution fusion | flops 3221225472 | bytes 6291456 | tf_op jit(solution)/shard_map/dot_general | solution.py:139
  219.1 1.3 copy.78
  (26 shorter events, 2.8 us)
Async XLA Ops:
  0.0 24.2 %copy-start = (bf16[128,16,128]{2,1,0:T(8,128)(2,1)S(1)}, bf16[128,16,128]{2,1,0:T(8,128)(2,1)}, u32[]{:S(2)}) copy-start(bf16[128,16,128]{2,1,0:T(8,128)(2,1)} %param.23) | copy-start | bytes 1572868
  3.1 27.1 %all-to-all-start = ((s32[128,1,2]{2,1,0:T(1,128)}), s32[128,1,2]{2,1,0:T(1,128)S(1)}, u32[]{:S(2)}, u32[]{:S(2)}) async-start(s32[128,1,2]{2,1,0:T(1,128)} %bitcast.1), calls=%async_computation | async-start | bytes 131072 | tf_op jit(solution)/shard_map/all_to_all | solution.py:104
  30.3 40.3 %all-to-all-start.1 = ((bf16[128,2,4096]{2,1,0:T(2,128)(2,1)}), bf16[128,2,4096]{2,1,0:T(2,128)(2,1)S(1)}, u32[]{:S(2)}, u32[]{:S(2)}) async-start(bf16[128,2,4096]{2,1,0:T(2,128)(2,1)} %reshape.218), calls=%async_computation.1 | async-start | bytes 4194304 | tf_op jit(solution)/shard_map/all_to_all | solution.py:97
  104.4 8.8 %copy-start.4 = (pred[2]{0:T(512)(128)(4,1)S(1)}, pred[2]{0:T(512)(128)(4,1)}, u32[]{:S(2)}) copy-start(pred[2]{0:T(512)(128)(4,1)} %constant.207.clone.1) | copy-start | bytes 10
  104.4 10.2 %copy-start.2 = (f32[16,9,8,33,8]{0,4,3,2,1:T(8,128)S(1)}, f32[16,9,8,33,8]{0,4,3,2,1:T(8,128)}, u32[]{:S(2)}) copy-start(f32[16,9,8,33,8]{0,4,3,2,1:T(8,128)} %copy.71) | copy-start | bytes 3649540
  108.9 4.1 %collective-permute-start = (bf16[16,2,264]{0,2,1:T(8,128)(2,1)S(1)}, bf16[16,2,264]{0,2,1:T(8,128)(2,1)S(1)}, u32[]{:S(2)}, u32[]{:S(2)}) collective-permute-start(bf16[16,2,264]{0,2,1:T(8,128)(2,1)S(1)} %slice.242), channel_id=1, source_target_pairs={{0,8},{8,16},{16,24},{24,32},{32,40},{40,48},{48,56},{56,64},{64,7... | collective-permute-start | bytes 50696 | tf_op jit(solution)/shard_map/ppermute | solution.py:18
  113.2 6.2 %collective-permute-start.1 = (bf16[16,2,264]{0,2,1:T(8,128)(2,1)S(1)}, bf16[16,2,264]{0,2,1:T(8,128)(2,1)S(1)}, u32[]{:S(2)}, u32[]{:S(2)}) collective-permute-start(bf16[16,2,264]{0,2,1:T(8,128)(2,1)S(1)} %get-tuple-element.107), channel_id=1, source_target_pairs={{8,0},{16,8},{24,16},{32,24},{40,32},{48,40},{56,48},{64,56},{72,6... | collective-permute-start | bytes 50696 | tf_op jit(solution)/shard_map/ppermute | solution.py:21
  122.9 8.1 %collective-permute-start.2 = (f32[16,64,2]{0,2,1:T(2,128)S(1)}, f32[16,64,2]{0,2,1:T(2,128)S(1)}, u32[]{:S(2)}, u32[]{:S(2)}) collective-permute-start(f32[16,64,2]{0,2,1:T(2,128)S(1)} %get-tuple-element.106), channel_id=1, source_target_pairs={{0,1},{1,2},{2,3},{3,4},{4,5},{5,6},{6,7},{7,0},{8,9},{9,10},{10,1... | collective-permute-start | bytes 24584 | tf_op jit(solution)/shard_map/ppermute | solution.py:18
  130.0 3.7 %collective-permute-start.3 = (f32[16,64,2]{0,2,1:T(2,128)S(1)}, f32[16,64,2]{0,2,1:T(2,128)S(1)}, u32[]{:S(2)}, u32[]{:S(2)}) collective-permute-start(f32[16,64,2]{0,2,1:T(2,128)S(1)} %get-tuple-element.105), channel_id=1, source_target_pairs={{1,0},{2,1},{3,2},{4,3},{5,4},{6,5},{7,6},{0,7},{9,8},{10,9},{11,1... | collective-permute-start | bytes 24584 | tf_op jit(solution)/shard_map/ppermute | solution.py:21
  132.0 3.2 %copy-start.3 = (f32[16,64,256]{0,2,1:T(8,128)}, f32[16,64,256]{0,2,1:T(8,128)S(1)}, u32[]{:S(2)}) copy-start(f32[16,64,256]{0,2,1:T(8,128)S(1)} %fusion.21) | copy-start | bytes 3145732
  203.4 17.0 %copy-start.1 = (bf16[128,16,128]{2,1,0:T(8,128)(2,1)S(1)}, bf16[128,16,128]{2,1,0:T(8,128)(2,1)}, u32[]{:S(2)}) copy-start(bf16[128,16,128]{2,1,0:T(8,128)(2,1)} %param.23) | copy-start | bytes 1572868
where the time goes:
time: 223 us; the launch traced here: 220 us
  local copies, waits for them, and re-layouts  55.1 us (25%)
  blocking collectives  42.5 us (19%)
  other arithmetic  36.6 us (16%)
  waiting for transfers between devices  33.6 us (15%)
  starting transfers between devices  28.1 us (13%)
  matrix products  24.2 us (11%)
    all_to_all x1, waiting for transfers between devices, on_device(): lax.all_to_all(packed.reshape(flat_shape + (chans * span * span,)), ('lat...  29 us
    all_to_all x1, blocking collectives, on_device(): lax.all_to_all(lon_adjoint, 'lat', split_axis=2, concat_axis=1, tiled=True)  22.1 us
    all_to_all x1, blocking collectives, on_device(): lines = lax.all_to_all(tile, 'lon', split_axis=0, concat_axis=2, tiled=True)  20.4 us
    dot_general x1, matrix products, on_device(): jnp.dot(lines.reshape(share * CLAT, lines.shape[2]), lon_inverse, precisi...  12.5 us
    all_to_all x1, starting transfers between devices, on_device(): lax.all_to_all(labels.reshape(flat_shape), ('lat', 'lon'), split_axis=0,...  11.5 us
    all_to_all x1, starting transfers between devices, on_device(): lax.all_to_all(packed.reshape(flat_shape + (chans * span * span,)), ('lat...  9.77 us
    transpose x1, local copies, waits for them, and re-layouts, on_device(): jnp.transpose(cols_done, (2, 0, 3, 1, 4))  8.88 us
    unnamed x16, local copies, waits for them, and re-layouts  8 us
  transfers between devices with their start and end apart: 6, of which 4 were waited for; matrix products, arithmetic and copies ran while one was open for 12% of the time, Pallas kernels for 0%

commit v1 on v0

v1 whole, which is shorter than its diff:
```python
import jax
import jax.numpy as jnp
from jax import lax
from jax.experimental import pallas as pl
from jax.experimental.pallas import tpu as pltpu
from jax.sharding import PartitionSpec as P

MESH = pl.DeviceIdType.MESH
F32 = jnp.float32
BF16 = jnp.bfloat16
LATS = 16
LONS = 8
BLOCKS = 128
CHANS = 16
NLAT = 1024
NLON = 2048
PAIR = 16
LABEL = 127
BANDS = 9
ROWS = BANDS * 16


def partner(step, lat, lon):
    turn, hop = step // LATS, step % LATS
    x = (lat // 4 + hop // 4) % 4
    y = (lat % 4 + hop % 4) % 4
    z = (lon // 2 + turn // 2) % 4
    core = (lon % 2 + turn % 2) % 2
    return x * 4 + y, z * 2 + core


def spline(distance):
    size = jnp.abs(distance)
    far = jnp.maximum(2.0 - size, 0.0)
    near = jnp.maximum(1.0 - size, 0.0)
    return far * far * far - 4.0 * (near * near * near)


def wait_for(view, sem):
    pltpu.make_async_copy(view, view, sem).wait()


def sublane_places(first):
    row = lax.broadcasted_iota(jnp.int32, (8, 128), 0)
    return jnp.where(row < 3, row + 8, first(row)).astype(F32)


def kernel(cot_ref, frac_ref, off_ref, owner_ref, sub_ref, lon_ref, lat_ref, out_ref,
           lat_tab, windows, packed, got, summed, coeff, lon_raw, lon_half, lat_raw, lat_high,
           lat_low, lines, columns, column_sum,
           ready_sem, load_sem, send_sem, recv_sem, line_send, line_recv):
    lat, lon = lax.axis_index("lat"), lax.axis_index("lon")
    barrier = pltpu.get_barrier_semaphore()

    def greet(step, carry):
        lat_to, lon_to = partner(step, lat, lon)
        pl.semaphore_signal(barrier, inc=1, device_id=(lat_to, lon_to), device_id_type=MESH)
        return carry

    lax.fori_loop(1, LATS, greet, 0)
    lax.fori_loop(1, LONS, lambda turn, carry: greet(turn * LATS, carry), 0)

    for part in range(16):
        pltpu.make_async_copy(
            lon_ref.at[:, pl.ds(part * 128, 128)], lon_raw.at[part], load_sem.at[0]
        ).start()
    pltpu.make_async_copy(lat_ref, lat_raw, load_sem.at[1]).start()

    index = lax.broadcasted_iota(jnp.int32, (8, 128), 0)
    low = index.astype(F32)
    low_tail = index < 3
    ends_a = sublane_places(lambda row: row - 3)
    ends_b = sublane_places(lambda row: row + 2)
    ends_c = sublane_places(lambda row: jnp.where(row < 6, 10, 15))
    lat_c = jnp.where(low_tail, 6, jnp.where(index < 6, index + 5, 15)).astype(F32)

    def window_group(group, carry):
        places = off_ref[pl.ds(group * 8, 8)].astype(F32) + 1.0 + frac_ref[pl.ds(group * 8, 8)]
        for item in range(8):
            block = group * 8 + item
            centre_lat = jnp.broadcast_to(places[item, 0:1, :], (8, 128))
            centre_lon = jnp.broadcast_to(places[item, 1:2, :], (8, 128))
            lat_tab[item, 0:8, :] = spline(low - centre_lat) * (1.0 / 36.0)
            lat_tab[item, 8:16, :] = spline(low + 8.0 - centre_lat) * (1.0 / 36.0)
            lat_last = spline(lat_c - centre_lat) * (1.0 / 36.0)
            lon_head = spline(low - centre_lon)
            tail_a = spline(ends_a - centre_lon)
            tail_b = spline(ends_b - centre_lon)
            tail_c = spline(ends_c - centre_lon)

            def lat_row(w):
                return jnp.broadcast_to(lat_tab[item, w : w + 1, :], (8, 128))

            high_rows = [lat_row(8), lat_row(9), lat_row(10)]
            pieces = []
            for w in range(8):
                row = lat_row(w)
                if w < 6:
                    tail_lat = jnp.where(low_tail, row, high_rows[w % 3])
                elif w == 6:
                    tail_lat = lat_last
                else:
                    tail_lat = row
                tail_lon = tail_a if w < 3 else (tail_b if w < 6 else tail_c)
                pieces.append(row * lon_head)
                pieces.append(tail_lat * tail_lon)
            stencil = jnp.concatenate(pieces, axis=0).astype(BF16)
            window = lax.dot_general(
                cot_ref[block], stencil, (((1,), (1,)), ((), ())), preferred_element_type=F32
            )
            windows[pl.ds(pl.multiple_of(block * CHANS, CHANS), CHANS), :] = window
        return carry

    lax.fori_loop(0, 8, window_group, 0)

    pl.semaphore_wait(barrier, LATS - 1 + LONS - 1)

    def tell(step, carry):
        lat_to, lon_to = partner(step, lat, lon)
        pl.semaphore_signal(ready_sem, inc=1, device_id=(lat_to, lon_to), device_id_type=MESH)
        return carry

    lax.fori_loop(1, LATS, tell, 0)
    lax.fori_loop(8, 16, window_group, 0)

    own_down = jnp.broadcast_to(owner_ref[...].astype(F32), (BLOCKS, BLOCKS))
    own_across = own_down.T
    down = lax.broadcasted_iota(jnp.int32, (BLOCKS, BLOCKS), 0)
    across = lax.broadcasted_iota(jnp.int32, (BLOCKS, BLOCKS), 1)
    earlier = jnp.where((own_down == own_across) & (down < across), 1.0, 0.0)
    place = 2.0 * own_across[0:1, :] + jnp.sum(earlier, axis=0, keepdims=True)
    slot = lax.broadcasted_iota(jnp.int32, (2 * BLOCKS, BLOCKS), 0).astype(F32)
    select = jnp.where(slot == place, 1.0, 0.0).astype(BF16)
    label = jnp.broadcast_to(sub_ref[...].astype(F32), (BLOCKS, BLOCKS)).T

    pl.semaphore_wait(ready_sem, LATS - 1)

    def send_group(turn, carry):
        _, lon_to = partner(turn * LATS, lat, lon)
        first = windows[pl.ds(2 * lon_to, BLOCKS, stride=CHANS), :]
        second = windows[pl.ds(2 * lon_to + 1, BLOCKS, stride=CHANS), :]
        first = jnp.where(across == LABEL, label, first)
        both = jnp.concatenate([first.astype(BF16), second.astype(BF16)], axis=1)
        packed[turn] = jnp.dot(select, both, preferred_element_type=F32).astype(BF16)

        def send(hop, inner):
            lat_to, lon_there = partner(turn * LATS + hop, lat, lon)
            pltpu.make_async_remote_copy(
                src_ref=packed.at[turn, pl.ds(pl.multiple_of(lat_to * PAIR, PAIR), PAIR)],
                dst_ref=got.at[turn * LATS + hop],
                send_sem=send_sem,
                recv_sem=recv_sem.at[turn],
                device_id=(lat_to, lon_there),
                device_id_type=MESH,
            ).start()
            return inner

        @pl.when(turn > 0)
        def _():
            send(0, 0)

        @pl.when(turn == 0)
        def _():
            got[0] = packed[0, pl.ds(pl.multiple_of(lat * PAIR, PAIR), PAIR), :]

        lax.fori_loop(1, LATS, send, 0)
        return carry

    lax.fori_loop(0, LONS, send_group, 0)

    summed[...] = jnp.zeros_like(summed)
    wait_for(lon_raw, load_sem.at[0])

    def prepare_lon(part, carry):
        for residue in range(8):
            rows = lon_raw[part, pl.ds(residue, 256, stride=8), :]
            lon_half[part, residue * 256 : (residue + 1) * 256, :] = rows.astype(BF16)
        return carry

    lax.fori_loop(0, 16, prepare_lon, 0)
    wait_for(lat_raw, load_sem.at[1])

    def prepare_lat(part, carry):
        start = pl.multiple_of(part * 128, 128)
        for piece in range(8):
            turned = lat_raw[pl.ds(start, 128), piece * 128 : (piece + 1) * 128].T
            high = turned.astype(BF16)
            lat_high[part, piece * 128 : (piece + 1) * 128, :] = high
            lat_low[part, piece * 128 : (piece + 1) * 128, :] = (
                turned - high.astype(F32)
            ).astype(BF16)
        return carry

    lax.fori_loop(0, 8, prepare_lat, 0)

    lanes = lax.broadcasted_iota(jnp.int32, (256, 256), 1).astype(F32)
    tile = (lax.broadcasted_iota(jnp.int32, (256, 1), 0) // 2) % 8

    def add_group(turn):
        view = got.at[pl.ds(turn * LATS, LATS)]
        if turn == 0:
            wait_for(got.at[pl.ds(1, LATS - 1)], recv_sem.at[0])
        else:
            wait_for(view, recv_sem.at[turn])
        chunk = got[turn * LATS : (turn + 1) * LATS].reshape(256, 256)
        name = chunk[:, LABEL : LABEL + 1].astype(F32).astype(jnp.int32)
        goal = ((name // 32) * 256 + tile * 32 + name % 32).astype(F32)
        goal = jnp.broadcast_to(goal, (256, 256)) - lanes
        turned = chunk.astype(F32).T.astype(BF16)
        for band in range(8):
            match = jnp.where(goal == float(band * 256), 1.0, 0.0).astype(BF16)
            add = jnp.dot(turned, match, preferred_element_type=F32)
            summed[2 * band + 2, 0:256, :] += add[:, :128]
            summed[2 * band + 3, 0:256, :] += add[:, 128:]

    for turn in range(LONS):
        add_group(turn)

    tail_mask = lax.broadcasted_iota(jnp.int32, (8, 256), 0) < 3

    def fold(band, carry):
        def rows(block, start, stride):
            return jnp.concatenate(
                [
                    summed[2 * block + half, pl.ds(start, 8, stride=stride), :]
                    for half in range(2)
                ],
                axis=1,
            )

        def column(chan, v):
            main = rows(band + 1, chan * 128 + v, 16)
            if v < 10:
                over = rows(band, chan * 128 + 11 + v % 5 + 48 * (v // 5), 16)
            else:
                over = rows(band, chan * 128 + 96 + 11, 1)
            return main + jnp.where(tail_mask, over, 0.0)

        def residue_of(chan, q):
            if q == 7:
                return column(chan, 8) + pltpu.roll(column(chan, 0), 255, 1)
            if q < 2:
                return column(chan, q + 1) + pltpu.roll(column(chan, q + 9), 1, 1)
            return column(chan, q + 1)

        for q in range(8):
            value = jnp.concatenate([residue_of(0, q), residue_of(1, q)], axis=0)
            high = value.astype(BF16)
            coeff[pl.ds(pl.multiple_of(band * 16, 16), 16), q * 256 : (q + 1) * 256] = high
            coeff[pl.ds(pl.multiple_of(ROWS + band * 16, 16), 16), q * 256 : (q + 1) * 256] = (
                value - high.astype(F32)
            ).astype(BF16)
        return carry

    lax.fori_loop(0, BANDS, fold, 0)

    def line_group(step, carry):
        group = (lat // 2 + step) % 8
        weights = jnp.concatenate([lon_half[2 * group], lon_half[2 * group + 1]], axis=1)
        product = jnp.dot(coeff[...], weights, preferred_element_type=F32)
        total = (product[:ROWS] + product[ROWS:]).astype(BF16)
        for half in range(2):
            there = 2 * group + half
            lines[there] = total[:, half * 128 : (half + 1) * 128]

            @pl.when(there != lat)
            def _():
                pltpu.make_async_remote_copy(
                    src_ref=lines.at[there],
                    dst_ref=columns.at[lat],
                    send_sem=line_send,
                    recv_sem=line_recv,
                    device_id=(there, lon),
                    device_id_type=MESH,
                ).start()

        return carry

    lax.fori_loop(1, 9, line_group, 0)
    wait_for(columns.at[pl.ds(0, LATS - 1)], line_recv)
    columns[lat] = lines[lat]

    def assemble(source, carry):
        before = jnp.maximum(source - 1, 0)
        tail = columns[before, 128:144, :].astype(F32)
        for band in range(8):
            value = columns[source, band * 16 : (band + 1) * 16, :].astype(F32)
            if band == 0:
                value = value + jnp.where(source > 0, tail, 0.0)
            start = pl.multiple_of(source * 64 + band * 8, 8)
            column_sum[pl.ds(start, 8), 0:128] = value[0:8]
            column_sum[pl.ds(start, 8), 128:256] = value[8:16]
        return carry

    lax.fori_loop(0, LATS, assemble, 0)
    last = columns[LATS - 1, 128:144, :].astype(F32)
    column_sum[NLAT : NLAT + 8, 0:128] = last[0:8]
    column_sum[NLAT : NLAT + 8, 128:256] = last[8:16]
    whole = column_sum[1 : NLAT + 1, :].astype(BF16)

    for piece in range(4):
        span = slice(piece * 256, (piece + 1) * 256)
        high = jnp.concatenate([lat_high[part, span, :] for part in range(8)], axis=1)
        low_part = jnp.concatenate([lat_low[part, span, :] for part in range(8)], axis=1)
        result = jnp.dot(high, whole, preferred_element_type=F32) + jnp.dot(
            low_part, whole, preferred_element_type=F32
        )
        out_ref[0, span, :] = result[:, :128]
        out_ref[1, span, :] = result[:, 128:]

    wait_for(got.at[pl.ds(0, LATS * LONS - 1)], send_sem)
    wait_for(lines.at[pl.ds(0, LATS - 1)], line_send)


def on_device(cotangent, fractions, offsets, owner, sub_block, lon_inverse, lat_inverse):
    vmem = pl.BlockSpec(memory_space=pltpu.VMEM)
    anywhere = pl.BlockSpec(memory_space=pl.ANY)
    return pl.pallas_call(
        kernel,
        out_shape=jax.ShapeDtypeStruct((2, NLAT, 128), F32),
        in_specs=[vmem] * 5 + [anywhere] * 2,
        out_specs=vmem,
        scratch_shapes=[
            pltpu.VMEM((8, 16, 128), F32),
            pltpu.VMEM((BLOCKS * CHANS, 128), F32),
            pltpu.VMEM((LONS, 256, 256), BF16),
            pltpu.VMEM((LATS * LONS, PAIR, 256), BF16),
            pltpu.VMEM((20, 320, 128), F32),
            pltpu.VMEM((2 * ROWS, NLON), BF16),
            pltpu.VMEM((16, NLON, 128), F32),
            pltpu.VMEM((16, NLON, 128), BF16),
            pltpu.VMEM((NLAT, NLAT), F32),
            pltpu.VMEM((8, NLAT, 128), BF16),
            pltpu.VMEM((8, NLAT, 128), BF16),
            pltpu.VMEM((LATS, ROWS, 128), BF16),
            pltpu.VMEM((LATS, ROWS, 128), BF16),
            pltpu.VMEM((NLAT + 8, 256), F32),
            pltpu.SemaphoreType.REGULAR,
            pltpu.SemaphoreType.DMA((2,)),
            pltpu.SemaphoreType.DMA,
            pltpu.SemaphoreType.DMA((LONS,)),
            pltpu.SemaphoreType.DMA,
            pltpu.SemaphoreType.DMA,
        ],
        compiler_params=pltpu.CompilerParams(
            collective_id=0, has_side_effects=True, vmem_limit_bytes=60 * 2**20
        ),
    )(cotangent, fractions, offsets, owner, sub_block.reshape(1, BLOCKS), lon_inverse, lat_inverse)


def solution(mesh):
    return jax.shard_map(
        on_device,
        mesh=mesh,
        in_specs=(
            P(("lat", "lon"), None, None),
            P(("lat", "lon"), None, None),
            P(("lat", "lon"), None, None),
            P(("lat", "lon"), None),
            P(("lat", "lon")),
            P(),
            P(),
        ),
        out_specs=P("lon", None, "lat"),
        check_vma=False,
    )
```

time: 223 us -> 50.1 us (0.22)
  local copies, waits for them, and re-layouts: 55.1 us -> 3.65 us
  Pallas kernels: 0 us -> 45.5 us
  blocking collectives: 42.5 us -> 0 us
  other arithmetic: 36.6 us -> 0 us
  waiting for transfers between devices: 33.6 us -> 0 us
  starting transfers between devices: 28.1 us -> 0 us
  matrix products: 24.2 us -> 0 us
    pallas_call x0 -> x1, Pallas kernels: none -> 45.5 us  [on_device(): pl.pallas_call(kernel, out_shape=jax.ShapeDtypeStruct((2, NLAT, 128), F32...]
    all_to_all x2 -> x0, blocking collectives: 42.5 us -> none  [the longest x1 22.1 us: on_device(): lax.all_to_all(lon_adjoint, 'lat', split_axis=2, concat_axis=1, tiled=True)]
    all_to_all x2 -> x0, waiting for transfers between devices: 29 us -> none  [the longest x1 29 us: on_device(): lax.all_to_all(packed.reshape(flat_shape + (chans * span * span,)), ('lat...]
    dot_general x5 -> x0, matrix products: 24.2 us -> none  [the longest x1 12.5 us: on_device(): jnp.dot(lines.reshape(share * CLAT, lines.shape[2]), lon_inverse, precisi...]
    all_to_all x2 -> x0, starting transfers between devices: 21.3 us -> none  [the longest x1 11.5 us: on_device(): lax.all_to_all(labels.reshape(flat_shape), ('lat', 'lon'), split_axis=0,...]
    transpose x2 -> x0, local copies, waits for them, and re-layouts: 10.2 us -> none  [the longest x1 8.88 us: on_device(): jnp.transpose(cols_done, (2, 0, 3, 1, 4))]
    slice x3 -> x0, local copies, waits for them, and re-layouts: 8.55 us -> none  [the longest x1 4.66 us: on_device(): tile = core[:, :, 1:CLON + 1]]
    scatter-add x2 -> x0, local copies, waits for them, and re-layouts: 7.07 us -> none  [on_device(): tile = tile.at[:, :, CLON - 1:CLON].add(lon_got[:, :, 6:7])]
  transfers between devices with their start and end apart: 6 -> 0, of which waited for: 4 -> 0; matrix products, arithmetic and copies ran while one was open for 12% -> 0% of each run, Pallas kernels for 0% -> 0%
where the time goes in v1:
time: 50.1 us; the launch traced here: 49.2 us
  Pallas kernels  45.5 us (91%)
  local copies, waits for them, and re-layouts  3.65 us (7%)
    pallas_call x1, Pallas kernels, on_device(): pl.pallas_call(kernel, out_shape=jax.ShapeDtypeStruct((2, NLAT, 128), F32...  45.5 us
    unnamed x2, local copies, waits for them, and re-layouts  3.65 us

profile of v1, /device:TPU:1, one launch (start us, length us, event | category | flops | bytes accessed | tf_op | source)
XLA Modules:
  0.0 49.2 jit_solution(14214304817912613210)
XLA Ops:
  0.0 1.4 %copy.8.owner_ref = s32[128,1]{1,0:T(8,128)} copy(s32[128,1]{0,1:T(1,128)} %param.10) | data formatting | bytes 1024 | tf_op args[3]
  1.4 45.5 %shard_map.73 = f32[2,1024,128]{2,1,0:T(8,128)} custom-call(bf16[128,16,128]{2,1,0:T(8,128)(2,1)} %cot_ref.1, f32[128,2,128]{2,1,0:T(2,128)} %frac_ref.1, s32[128,2,128]{2,1,0:T(2,128)} %off_ref.1, s32[128,1]{1,0:T(8,128)} %copy.8.owner_ref, s32[1,128]{1,0:T(1,128)} %bitcast.1, f32[2048,2048]{1,0:T(8,128)} %lon_ref.1, f32[1024,1024]{1,0:T(8,128)} %lat_ref.1), custom_call_target="tpu_custom_call" | custom-call | tf_op jit(solution)/shard_map/pallas_call | solution.py:318
  46.9 2.3 %copy.10 = f32[2,1024,128]{2,1,0:T(8,128)} copy(f32[2,1024,128]{2,1,0:T(8,128)} %shard_map.73) | data formatting | bytes 2097152

commit v2 on v1

--- a/solution.py
+++ b/solution.py
@@ -45,12 +45,26 @@
     return jnp.where(row < 3, row + 8, first(row)).astype(F32)
 
 
-def kernel(cot_ref, frac_ref, off_ref, owner_ref, sub_ref, lon_ref, lat_ref, out_ref,
-           lat_tab, windows, packed, got, summed, coeff, lon_raw, lon_half, lat_raw, lat_high,
+def kernel(cot_hbm, frac_hbm, off_hbm, owner_hbm, sub_hbm, lon_ref, lat_ref, out_ref,
+           cot_ref, frac_ref, off_ref, owner_ref, sub_ref, lat_tab, windows, packed, got, summed, coeff, lon_raw, lon_half, lat_raw, lat_high,
            lat_low, lines, columns, column_sum,
            ready_sem, load_sem, send_sem, recv_sem, line_send, line_recv):
     lat, lon = lax.axis_index("lat"), lax.axis_index("lon")
     barrier = pltpu.get_barrier_semaphore()
+    inputs = [
+        pltpu.make_async_copy(source, target, load_sem.at[2 + place])
+        for place, (source, target) in enumerate(
+            (
+                (cot_hbm, cot_ref),
+                (frac_hbm, frac_ref),
+                (off_hbm, off_ref),
+                (owner_hbm, owner_ref),
+                (sub_hbm, sub_ref),
+            )
+        )
+    ]
+    for copy in inputs:
+        copy.start()
 
     def greet(step, carry):
         lat_to, lon_to = partner(step, lat, lon)
@@ -65,6 +79,9 @@
             lon_ref.at[:, pl.ds(part * 128, 128)], lon_raw.at[part], load_sem.at[0]
         ).start()
     pltpu.make_async_copy(lat_ref, lat_raw, load_sem.at[1]).start()
+
+    for copy in inputs:
+        copy.wait()
 
     index = lax.broadcasted_iota(jnp.int32, (8, 128), 0)
     low = index.astype(F32)
@@ -111,7 +128,7 @@
             windows[pl.ds(pl.multiple_of(block * CHANS, CHANS), CHANS), :] = window
         return carry
 
-    lax.fori_loop(0, 8, window_group, 0)
+    lax.fori_loop(0, 12, window_group, 0)
 
     pl.semaphore_wait(barrier, LATS - 1 + LONS - 1)
 
@@ -120,11 +137,11 @@
         pl.semaphore_signal(ready_sem, inc=1, device_id=(lat_to, lon_to), device_id_type=MESH)
         return carry
 
-    lax.fori_loop(1, LATS, tell, 0)
-    lax.fori_loop(8, 16, window_group, 0)
-
-    own_down = jnp.broadcast_to(owner_ref[...].astype(F32), (BLOCKS, BLOCKS))
-    own_across = own_down.T
+    lax.fori_loop(1, LONS, lambda turn, carry: tell(turn * LATS, carry), 0)
+    lax.fori_loop(12, 16, window_group, 0)
+
+    own_across = jnp.broadcast_to(owner_ref[...].astype(F32), (BLOCKS, BLOCKS))
+    own_down = own_across.T
     down = lax.broadcasted_iota(jnp.int32, (BLOCKS, BLOCKS), 0)
     across = lax.broadcasted_iota(jnp.int32, (BLOCKS, BLOCKS), 1)
     earlier = jnp.where((own_down == own_across) & (down < across), 1.0, 0.0)
@@ -132,8 +149,6 @@
     slot = lax.broadcasted_iota(jnp.int32, (2 * BLOCKS, BLOCKS), 0).astype(F32)
     select = jnp.where(slot == place, 1.0, 0.0).astype(BF16)
     label = jnp.broadcast_to(sub_ref[...].astype(F32), (BLOCKS, BLOCKS)).T
-
-    pl.semaphore_wait(ready_sem, LATS - 1)
 
     def send_group(turn, carry):
         _, lon_to = partner(turn * LATS, lat, lon)
@@ -155,18 +170,16 @@
             ).start()
             return inner
 
-        @pl.when(turn > 0)
-        def _():
-            send(0, 0)
-
-        @pl.when(turn == 0)
-        def _():
+        if isinstance(turn, int):
             got[0] = packed[0, pl.ds(pl.multiple_of(lat * PAIR, PAIR), PAIR), :]
-
-        lax.fori_loop(1, LATS, send, 0)
-        return carry
-
-    lax.fori_loop(0, LONS, send_group, 0)
+            lax.fori_loop(1, LATS, send, 0)
+        else:
+            lax.fori_loop(0, LATS, send, 0)
+        return carry
+
+    send_group(0, 0)
+    pl.semaphore_wait(ready_sem, LONS - 1)
+    lax.fori_loop(1, LONS, send_group, 0)
 
     summed[...] = jnp.zeros_like(summed)
     wait_for(lon_raw, load_sem.at[0])
@@ -314,13 +327,22 @@
 
 def on_device(cotangent, fractions, offsets, owner, sub_block, lon_inverse, lat_inverse):
     vmem = pl.BlockSpec(memory_space=pltpu.VMEM)
-    anywhere = pl.BlockSpec(memory_space=pl.ANY)
+    hbm = pl.BlockSpec(memory_space=pltpu.HBM)
+    operands = (
+        cotangent, fractions, offsets, owner.reshape(1, BLOCKS), sub_block.reshape(1, BLOCKS),
+        lon_inverse, lat_inverse,
+    )
     return pl.pallas_call(
         kernel,
         out_shape=jax.ShapeDtypeStruct((2, NLAT, 128), F32),
-        in_specs=[vmem] * 5 + [anywhere] * 2,
+        in_specs=[hbm] * 7,
         out_specs=vmem,
         scratch_shapes=[
+            pltpu.VMEM((BLOCKS, CHANS, 128), BF16),
+            pltpu.VMEM((BLOCKS, 2, 128), F32),
+            pltpu.VMEM((BLOCKS, 2, 128), jnp.int32),
+            pltpu.VMEM((1, BLOCKS), jnp.int32),
+            pltpu.VMEM((1, BLOCKS), jnp.int32),
             pltpu.VMEM((8, 16, 128), F32),
             pltpu.VMEM((BLOCKS * CHANS, 128), F32),
             pltpu.VMEM((LONS, 256, 256), BF16),
@@ -336,16 +358,16 @@
             pltpu.VMEM((LATS, ROWS, 128), BF16),
             pltpu.VMEM((NLAT + 8, 256), F32),
             pltpu.SemaphoreType.REGULAR,
-            pltpu.SemaphoreType.DMA((2,)),
+            pltpu.SemaphoreType.DMA((7,)),
             pltpu.SemaphoreType.DMA,
             pltpu.SemaphoreType.DMA((LONS,)),
             pltpu.SemaphoreType.DMA,
             pltpu.SemaphoreType.DMA,
         ],
         compiler_params=pltpu.CompilerParams(
-            collective_id=0, has_side_effects=True, vmem_limit_bytes=60 * 2**20
+            collective_id=0, has_side_effects=True, vmem_limit_bytes=50 * 2**20
         ),
-    )(cotangent, fractions, offsets, owner, sub_block.reshape(1, BLOCKS), lon_inverse, lat_inverse)
+    )(*(pltpu.with_memory_space_constraint(value, pltpu.HBM) for value in operands))
 
 
 def solution(mesh):

time: 50.1 us -> 44.8 us (0.89)
  local copies, waits for them, and re-layouts: 3.65 us -> 0.97 us
  Pallas kernels: 45.5 us -> 43.3 us
    unnamed x2 -> x1, local copies, waits for them, and re-layouts: 3.65 us -> 0.97 us
    pallas_call x1, Pallas kernels: 45.5 us -> 43.3 us  [on_device(): pl.pallas_call(kernel, out_shape=jax.ShapeDtypeStruct((2, NLAT, 128), F32...]
where the time goes in v2:
time: 44.8 us; the launch traced here: 44.3 us
  Pallas kernels  43.3 us (97%)
  local copies, waits for them, and re-layouts  0.97 us (2%)
    pallas_call x1, Pallas kernels, on_device(): pl.pallas_call(kernel, out_shape=jax.ShapeDtypeStruct((2, NLAT, 128), F32...  43.3 us
    unnamed x1, local copies, waits for them, and re-layouts  0.97 us

profile of v2, /device:TPU:1, one launch (start us, length us, event | category | flops | bytes accessed | tf_op | source)
XLA Modules:
  0.0 44.3 jit_solution(10128166200116929978)
XLA Ops:
  0.0 43.3 %shard_map.73 = f32[2,1024,128]{2,1,0:T(8,128)S(1)} custom-call(bf16[128,16,128]{2,1,0:T(8,128)(2,1)} %cot_hbm.1, f32[128,2,128]{2,1,0:T(2,128)} %frac_hbm.1, s32[128,2,128]{2,1,0:T(2,128)} %off_hbm.1, s32[1,128]{1,0:T(1,128)} %bitcast.2, s32[1,128]{1,0:T(1,128)} %bitcast.3, f32[2048,2048]{1,0:T(8,128)} %lon_ref.1, f32[1024,1024]{1,0:T(8,128)} %lat_ref.1), custom_call_target="tpu_custom_call" | custom-call | tf_op jit(solution)/shard_map/pallas_call | solution.py:335
  43.3 1.0 %copy.9 = f32[2,1024,128]{2,1,0:T(8,128)} copy(f32[2,1024,128]{2,1,0:T(8,128)S(1)} %shard_map.73) | data formatting | bytes 2097152

commit v3 on v2

v3 whole, which is shorter than its diff:
```python
import jax
import jax.numpy as jnp
from jax import lax
from jax.experimental import pallas as pl
from jax.experimental.pallas import tpu as pltpu
from jax.sharding import PartitionSpec as P

MESH = pl.DeviceIdType.MESH
F32 = jnp.float32
BF16 = jnp.bfloat16
LATS = 16
LONS = 8
BLOCKS = 128
CHANS = 16
NLAT = 1024
NLON = 2048
PAIR = 16
LABEL = 127
ROWS = 80
SELF = 8
STEPS = LATS * LONS


def spline(distance):
    size = jnp.abs(distance)
    far = jnp.maximum(2.0 - size, 0.0)
    near = jnp.maximum(1.0 - size, 0.0)
    return far * far * far - 4.0 * (near * near * near)


def wait_for(view, sem):
    pltpu.make_async_copy(view, view, sem).wait()


def sublane_places(first):
    row = lax.broadcasted_iota(jnp.int32, (8, 128), 0)
    return jnp.where(row < 3, row + 8, first(row)).astype(F32)


def kernel(cot_hbm, frac_hbm, off_hbm, owner_hbm, sub_hbm, lon_ref, lat_ref, out_ref,
           cot_ref, frac_ref, off_ref, owner_ref, sub_ref, lat_tab, windows, packed, got, summed, coeff, lon_raw, lon_half, lat_raw, lat_high,
           lat_low, lines, columns, column_sum,
           ready_sem, load_sem, send_sem, recv_sem, line_send, line_recv):
    lat, lon = lax.axis_index("lat"), lax.axis_index("lon")
    barrier = pltpu.get_barrier_semaphore()
    inputs = [
        pltpu.make_async_copy(source, target, load_sem.at[2 + place])
        for place, (source, target) in enumerate(
            (
                (cot_hbm, cot_ref),
                (frac_hbm, frac_ref),
                (off_hbm, off_ref),
                (owner_hbm, owner_ref),
                (sub_hbm, sub_ref),
            )
        )
    ]
    for copy in inputs:
        copy.start()

    lat_others = [
        (lat // 4 + dx) % 4 * 4 + (lat % 4 + dy) % 4
        for dx in range(4)
        for dy in range(4)
        if dx + dy > 0
    ]
    lon_there = [(lon // 2 + turn // 2) % 4 * 2 + (lon % 2 + turn % 2) % 2 for turn in range(8)]

    def greet(sem, lat_to, lon_to):
        pl.semaphore_signal(sem, inc=1, device_id=(lat_to, lon_to), device_id_type=MESH)

    for lat_to in lat_others:
        greet(barrier, lat_to, lon)
    for lon_to in lon_there[1:]:
        greet(barrier, lat, lon_to)

    for part in range(16):
        pltpu.make_async_copy(
            lon_ref.at[:, pl.ds(part * 128, 128)], lon_raw.at[part], load_sem.at[0]
        ).start()
    pltpu.make_async_copy(lat_ref, lat_raw, load_sem.at[1]).start()

    for copy in inputs:
        copy.wait()

    index = lax.broadcasted_iota(jnp.int32, (8, 128), 0)
    low = index.astype(F32)
    low_tail = index < 3
    ends_a = sublane_places(lambda row: row - 3)
    ends_b = sublane_places(lambda row: row + 2)
    ends_c = sublane_places(lambda row: jnp.where(row < 6, 10, 15))
    lat_c = jnp.where(low_tail, 6, jnp.where(index < 6, index + 5, 15)).astype(F32)

    def window_group(group, carry):
        places = off_ref[pl.ds(group * 8, 8)].astype(F32) + 1.0 + frac_ref[pl.ds(group * 8, 8)]
        for item in range(8):
            block = group * 8 + item
            centre_lat = jnp.broadcast_to(places[item, 0:1, :], (8, 128))
            centre_lon = jnp.broadcast_to(places[item, 1:2, :], (8, 128))
            lat_tab[item, 0:8, :] = spline(low - centre_lat) * (1.0 / 36.0)
            lat_tab[item, 8:16, :] = spline(low + 8.0 - centre_lat) * (1.0 / 36.0)
            lat_last = spline(lat_c - centre_lat) * (1.0 / 36.0)
            lon_head = spline(low - centre_lon)
            tail_a = spline(ends_a - centre_lon)
            tail_b = spline(ends_b - centre_lon)
            tail_c = spline(ends_c - centre_lon)

            def lat_row(w):
                return jnp.broadcast_to(lat_tab[item, w : w + 1, :], (8, 128))

            high_rows = [lat_row(8), lat_row(9), lat_row(10)]
            pieces = []
            for w in range(8):
                row = lat_row(w)
                if w < 6:
                    tail_lat = jnp.where(low_tail, row, high_rows[w % 3])
                elif w == 6:
                    tail_lat = lat_last
                else:
                    tail_lat = row
                tail_lon = tail_a if w < 3 else (tail_b if w < 6 else tail_c)
                pieces.append(row * lon_head)
                pieces.append(tail_lat * tail_lon)
            stencil = jnp.concatenate(pieces, axis=0).astype(BF16)
            window = lax.dot_general(
                cot_ref[block], stencil, (((1,), (1,)), ((), ())), preferred_element_type=F32
            )
            windows[pl.ds(pl.multiple_of(block * CHANS, CHANS), CHANS), :] = window
        return carry

    lax.fori_loop(0, 12, window_group, 0)

    pl.semaphore_wait(barrier, LATS - 1 + LONS - 1)

    for lon_to in lon_there[1:]:
        greet(ready_sem, lat, lon_to)
    lax.fori_loop(12, 16, window_group, 0)

    own_across = jnp.broadcast_to(owner_ref[...].astype(F32), (BLOCKS, BLOCKS))
    own_down = own_across.T
    down = lax.broadcasted_iota(jnp.int32, (BLOCKS, BLOCKS), 0)
    across = lax.broadcasted_iota(jnp.int32, (BLOCKS, BLOCKS), 1)
    earlier = jnp.where((own_down == own_across) & (down < across), 1.0, 0.0)
    place = 2.0 * own_across[0:1, :] + jnp.sum(earlier, axis=0, keepdims=True)
    slot = lax.broadcasted_iota(jnp.int32, (2 * BLOCKS, BLOCKS), 0).astype(F32)
    select = jnp.where(slot == place, 1.0, 0.0).astype(BF16)
    label = jnp.broadcast_to(sub_ref[...].astype(F32), (BLOCKS, BLOCKS)).T

    def pack(chan):
        for pair in range(0, LONS, 2):
            sides = []
            for lon_to in (pair, pair + 1):
                window = windows[pl.ds(2 * lon_to + chan, BLOCKS, stride=CHANS), :]
                sides.append(jnp.where(across == LABEL, label, window).astype(BF16))
            both = jnp.concatenate(sides, axis=1)
            slots = jnp.dot(select, both, preferred_element_type=F32).astype(BF16)
            packed[chan, pair] = slots[:, :128]
            packed[chan, pair + 1] = slots[:, 128:]
        start = pl.multiple_of(lat * PAIR, PAIR)
        got[chan, SELF] = packed[chan, lon, pl.ds(start, PAIR), :]

    def send_group(chan):
        def body(group, carry):
            for half in range(2):
                x = (lat // 4 + group // 4 + 2 - 2 * half) % 4
                y = (lat % 4 + group % 4 + 2 - 2 * half) % 4
                lat_to = x * 4 + y
                start = pl.multiple_of(lat_to * PAIR, PAIR)
                for turn in range(8):
                    step = group * 16 + half * 8 + turn
                    copy = pltpu.make_async_remote_copy(
                        src_ref=packed.at[chan, lon_there[turn], pl.ds(start, PAIR)],
                        dst_ref=got.at[chan, step],
                        send_sem=send_sem.at[chan],
                        recv_sem=recv_sem.at[chan * 8 + group],
                        device_id=(lat_to, lon_there[turn]),
                        device_id_type=MESH,
                    )
                    if half * 8 + turn == SELF:
                        pl.when(group > 0)(copy.start)
                    else:
                        copy.start()
            return carry

        return body

    pack(0)
    pl.semaphore_wait(ready_sem, LONS - 1)
    lax.fori_loop(0, 8, send_group(0), 0)
    pack(1)

    wait_for(lon_raw, load_sem.at[0])

    def prepare_lon(part, carry):
        for residue in range(8):
            rows = lon_raw[part, pl.ds(residue, 256, stride=8), :]
            lon_half[part, residue * 256 : (residue + 1) * 256, :] = rows.astype(BF16)
        return carry

    lax.fori_loop(0, 16, prepare_lon, 0)
    summed[...] = jnp.zeros_like(summed)

    def prepare_lat(part, carry):
        start = pl.multiple_of(part * 128, 128)
        for piece in range(8):
            turned = lat_raw[pl.ds(start, 128), piece * 128 : (piece + 1) * 128].T
            high = turned.astype(BF16)
            lat_high[part, piece * 128 : (piece + 1) * 128, :] = high
            lat_low[part, piece * 128 : (piece + 1) * 128, :] = (
                turned - high.astype(F32)
            ).astype(BF16)
        return carry

    lanes = lax.broadcasted_iota(jnp.int32, (256, 256), 1).astype(F32)
    tile = (lax.broadcasted_iota(jnp.int32, (256, 1), 0) // 2) % 8

    def add_group(chan, group):
        if group == 0:
            wait_for(got.at[chan, pl.ds(0, 15)], recv_sem.at[chan * 8])
        else:
            wait_for(got.at[chan, pl.ds(group * 16, 16)], recv_sem.at[chan * 8 + group])
        chunk = got[chan, group * 16 : (group + 1) * 16].reshape(256, 128)
        name = chunk[:, LABEL : LABEL + 1].astype(F32).astype(jnp.int32)
        goal = ((name // 32) * 256 + tile * 32 + name % 32).astype(F32)
        goal = jnp.broadcast_to(goal, (256, 256)) - lanes
        turned = chunk.astype(F32).T.astype(BF16)
        for band in range(8):
            match = jnp.where(goal == float(band * 256), 1.0, 0.0).astype(BF16)
            add = jnp.dot(turned, match, preferred_element_type=F32)
            summed[chan, 2 * band + 2, 0:128, :] += add[:, :128]
            summed[chan, 2 * band + 3, 0:128, :] += add[:, 128:]

    tail_mask = lax.broadcasted_iota(jnp.int32, (8, 256), 0) < 3

    def fold(chan):
        def rows(block, start, stride):
            return jnp.concatenate(
                [
                    summed[chan, 2 * block + half, pl.ds(start, 8, stride=stride), :]
                    for half in range(2)
                ],
                axis=1,
            )

        def fold_pair(pair, carry):
            def column(band, v):
                main = rows(band + 1, v, 16)
                if v < 10:
                    over = rows(band, 11 + v % 5 + 48 * (v // 5), 16)
                else:
                    over = rows(band, 96 + 11, 1)
                return main + jnp.where(tail_mask, over, 0.0)

            def residue_of(band, q):
                if q == 7:
                    return column(band, 8) + pltpu.roll(column(band, 0), 255, 1)
                if q < 2:
                    return column(band, q + 1) + pltpu.roll(column(band, q + 9), 1, 1)
                return column(band, q + 1)

            for q in range(8):
                value = jnp.concatenate(
                    [residue_of(2 * pair, q), residue_of(2 * pair + 1, q)], axis=0
                )
                high = value.astype(BF16)
                span = slice(q * 256, (q + 1) * 256)
                coeff[chan, pl.ds(pl.multiple_of(pair * 16, 16), 16), span] = high
                coeff[chan, pl.ds(pl.multiple_of(ROWS + pair * 16, 16), 16), span] = (
                    value - high.astype(F32)
                ).astype(BF16)
            return carry

        lax.fori_loop(0, 5, fold_pair, 0)

    def send_lines(chan):
        def line_group(step, carry):
            group = (lat // 2 + step) % 8
            weights = jnp.concatenate([lon_half[2 * group], lon_half[2 * group + 1]], axis=1)
            product = jnp.dot(coeff[chan], weights, preferred_element_type=F32)
            total = (product[:ROWS] + product[ROWS:]).astype(BF16)
            for half in range(2):
                there = 2 * group + half
                lines[chan, there] = total[:, half * 128 : (half + 1) * 128]

                @pl.when(there != lat)
                def _():
                    pltpu.make_async_remote_copy(
                        src_ref=lines.at[chan, there],
                        dst_ref=columns.at[chan, lat],
                        send_sem=line_send.at[chan],
                        recv_sem=line_recv.at[chan],
                        device_id=(there, lon),
                        device_id_type=MESH,
                    ).start()

            return carry

        lax.fori_loop(1, 9, line_group, 0, unroll=2)

    def finish(chan):
        wait_for(columns.at[chan, pl.ds(0, LATS - 1)], line_recv.at[chan])
        columns[chan, lat] = lines[chan, lat]

        def assemble(source, carry):
            before = jnp.maximum(source - 1, 0)
            tail = columns[chan, before, 64:80, :].astype(F32)[0:8]
            for pair in range(4):
                value = columns[chan, source, pair * 16 : (pair + 1) * 16, :].astype(F32)
                start = pl.multiple_of(source * 64 + pair * 16, 16)
                if pair == 0:
                    column_sum[pl.ds(start, 8), :] = value[0:8] + jnp.where(source > 0, tail, 0.0)
                    column_sum[pl.ds(start + 8, 8), :] = value[8:16]
                else:
                    column_sum[pl.ds(start, 16), :] = value
            return carry

        lax.fori_loop(0, LATS, assemble, 0)
        column_sum[NLAT : NLAT + 8, :] = columns[chan, LATS - 1, 64:80, :].astype(F32)[0:8]
        whole = column_sum[1 : NLAT + 1, :].astype(BF16)
        for piece in range(4):
            span = slice(piece * 256, (piece + 1) * 256)
            high = jnp.concatenate([lat_high[part, span, :] for part in range(8)], axis=1)
            low_part = jnp.concatenate([lat_low[part, span, :] for part in range(8)], axis=1)
            out_ref[chan, span, :] = jnp.dot(high, whole, preferred_element_type=F32) + jnp.dot(
                low_part, whole, preferred_element_type=F32
            )

    wait_for(lat_raw, load_sem.at[1])
    lax.fori_loop(0, 8, prepare_lat, 0)
    lax.fori_loop(0, 8, send_group(1), 0)
    for group in range(8):
        add_group(0, group)
    fold(0)
    send_lines(0)
    for group in range(8):
        add_group(1, group)
    fold(1)
    send_lines(1)
    finish(0)
    finish(1)

    for chan in range(2):
        wait_for(got.at[chan, pl.ds(0, STEPS - 1)], send_sem.at[chan])
        wait_for(lines.at[chan, pl.ds(0, LATS - 1)], line_send.at[chan])


def on_device(cotangent, fractions, offsets, owner, sub_block, lon_inverse, lat_inverse):
    vmem = pl.BlockSpec(memory_space=pltpu.VMEM)
    hbm = pl.BlockSpec(memory_space=pltpu.HBM)
    operands = (
        cotangent, fractions, offsets, owner.reshape(1, BLOCKS), sub_block.reshape(1, BLOCKS),
        lon_inverse, lat_inverse,
    )
    return pl.pallas_call(
        kernel,
        out_shape=jax.ShapeDtypeStruct((2, NLAT, 128), F32),
        in_specs=[hbm] * 7,
        out_specs=vmem,
        scratch_shapes=[
            pltpu.VMEM((BLOCKS, CHANS, 128), BF16),
            pltpu.VMEM((BLOCKS, 2, 128), F32),
            pltpu.VMEM((BLOCKS, 2, 128), jnp.int32),
            pltpu.VMEM((1, BLOCKS), jnp.int32),
            pltpu.VMEM((1, BLOCKS), jnp.int32),
            pltpu.VMEM((8, 16, 128), F32),
            pltpu.VMEM((BLOCKS * CHANS, 128), F32),
            pltpu.VMEM((2, LONS, 256, 128), BF16),
            pltpu.VMEM((2, STEPS, PAIR, 128), BF16),
            pltpu.VMEM((2, 22, 176, 128), F32),
            pltpu.VMEM((2, 2 * ROWS, NLON), BF16),
            pltpu.VMEM((16, NLON, 128), F32),
            pltpu.VMEM((16, NLON, 128), BF16),
            pltpu.VMEM((NLAT, NLAT), F32),
            pltpu.VMEM((8, NLAT, 128), BF16),
            pltpu.VMEM((8, NLAT, 128), BF16),
            pltpu.VMEM((2, LATS, ROWS, 128), BF16),
            pltpu.VMEM((2, LATS, ROWS, 128), BF16),
            pltpu.VMEM((NLAT + 8, 128), F32),
            pltpu.SemaphoreType.REGULAR,
            pltpu.SemaphoreType.DMA((7,)),
            pltpu.SemaphoreType.DMA((2,)),
            pltpu.SemaphoreType.DMA((16,)),
            pltpu.SemaphoreType.DMA((2,)),
            pltpu.SemaphoreType.DMA((2,)),
        ],
        compiler_params=pltpu.CompilerParams(
            collective_id=0, has_side_effects=True, vmem_limit_bytes=50 * 2**20
        ),
    )(*(pltpu.with_memory_space_constraint(value, pltpu.HBM) for value in operands))


def solution(mesh):
    return jax.shard_map(
        on_device,
        mesh=mesh,
        in_specs=(
            P(("lat", "lon"), None, None),
            P(("lat", "lon"), None, None),
            P(("lat", "lon"), None, None),
            P(("lat", "lon"), None),
            P(("lat", "lon")),
            P(),
            P(),
        ),
        out_specs=P("lon", None, "lat"),
        check_vma=False,
    )
```

time: 44.8 us -> 41.9 us (0.935); the launches traced: 44.3 us -> 41.8 us
  Pallas kernels: 43.3 us -> 40.9 us
    pallas_call x1, Pallas kernels: 43.3 us -> 40.9 us  [on_device(): pl.pallas_call(kernel, out_shape=jax.ShapeDtypeStruct((2, NLAT, 128), F32...]
where the time goes in v3:
time: 41.9 us; the launch traced here: 41.8 us
  Pallas kernels  40.9 us (98%)
  local copies, waits for them, and re-layouts  0.97 us (2%)
    pallas_call x1, Pallas kernels, on_device(): pl.pallas_call(kernel, out_shape=jax.ShapeDtypeStruct((2, NLAT, 128), F32...  40.9 us
    unnamed x1, local copies, waits for them, and re-layouts  0.97 us

profile of v3, /device:TPU:1, one launch (start us, length us, event | category | flops | bytes accessed | tf_op | source)
XLA Modules:
  0.0 41.8 jit_solution(13757893639698976238)
XLA Ops:
  0.0 40.9 %shard_map.73 = f32[2,1024,128]{2,1,0:T(8,128)S(1)} custom-call(bf16[128,16,128]{2,1,0:T(8,128)(2,1)} %cot_hbm.1, f32[128,2,128]{2,1,0:T(2,128)} %frac_hbm.1, s32[128,2,128]{2,1,0:T(2,128)} %off_hbm.1, s32[1,128]{1,0:T(1,128)} %bitcast.2, s32[1,128]{1,0:T(1,128)} %bitcast.3, f32[2048,2048]{1,0:T(8,128)} %lon_ref.1, f32[1024,1024]{1,0:T(8,128)} %lat_ref.1), custom_call_target="tpu_custom_call" | custom-call | tf_op jit(solution)/shard_map/pallas_call | solution.py:354
  40.9 1.0 %copy.9 = f32[2,1024,128]{2,1,0:T(8,128)} copy(f32[2,1024,128]{2,1,0:T(8,128)S(1)} %shard_map.73) | data formatting | bytes 2097152

commit v4 on v3

--- a/solution.py
+++ b/solution.py
@@ -212,23 +212,27 @@
         return carry
 
     lanes = lax.broadcasted_iota(jnp.int32, (256, 256), 1).astype(F32)
-    tile = (lax.broadcasted_iota(jnp.int32, (256, 1), 0) // 2) % 8
+    tile = (lax.broadcasted_iota(jnp.int32, (256, 1), 0) // 2) % 4
 
     def add_group(chan, group):
+        first = 32 * group
         if group == 0:
             wait_for(got.at[chan, pl.ds(0, 15)], recv_sem.at[chan * 8])
         else:
-            wait_for(got.at[chan, pl.ds(group * 16, 16)], recv_sem.at[chan * 8 + group])
-        chunk = got[chan, group * 16 : (group + 1) * 16].reshape(256, 128)
-        name = chunk[:, LABEL : LABEL + 1].astype(F32).astype(jnp.int32)
-        goal = ((name // 32) * 256 + tile * 32 + name % 32).astype(F32)
-        goal = jnp.broadcast_to(goal, (256, 256)) - lanes
-        turned = chunk.astype(F32).T.astype(BF16)
-        for band in range(8):
-            match = jnp.where(goal == float(band * 256), 1.0, 0.0).astype(BF16)
-            add = jnp.dot(turned, match, preferred_element_type=F32)
-            summed[chan, 2 * band + 2, 0:128, :] += add[:, :128]
-            summed[chan, 2 * band + 3, 0:128, :] += add[:, 128:]
+            wait_for(got.at[chan, pl.ds(first, 16)], recv_sem.at[chan * 8 + 2 * group])
+        wait_for(got.at[chan, pl.ds(first + 16, 16)], recv_sem.at[chan * 8 + 2 * group + 1])
+        chunk = got[chan, first : first + 32].astype(F32)
+        for half in range(2):
+            part = chunk[:, 8 * half : 8 * half + 8, :].reshape(256, 128)
+            name = part[:, LABEL : LABEL + 1].astype(jnp.int32)
+            goal = ((name // 32) * 128 + tile * 32 + name % 32).astype(F32)
+            goal = jnp.broadcast_to(goal, (256, 256)) - lanes
+            turned = part.T.astype(BF16)
+            for pair in range(4):
+                match = jnp.where(goal == float(pair * 256), 1.0, 0.0).astype(BF16)
+                add = jnp.dot(turned, match, preferred_element_type=F32)
+                summed[chan, 4 * pair + 2 + half, 0:128, :] += add[:, :128]
+                summed[chan, 4 * pair + 4 + half, 0:128, :] += add[:, 128:]
 
     tail_mask = lax.broadcasted_iota(jnp.int32, (8, 256), 0) < 3
 
@@ -274,28 +278,30 @@
 
     def send_lines(chan):
         def line_group(step, carry):
-            group = (lat // 2 + step) % 8
-            weights = jnp.concatenate([lon_half[2 * group], lon_half[2 * group + 1]], axis=1)
+            x, y = lat // 4 + step // 4, lat % 4 + step % 4
+            far = (x + 2) % 4 * 4 + (y + 2) % 4
+            near = x % 4 * 4 + y % 4
+            weights = jnp.concatenate([lon_half[far], lon_half[near]], axis=1)
             product = jnp.dot(coeff[chan], weights, preferred_element_type=F32)
             total = (product[:ROWS] + product[ROWS:]).astype(BF16)
-            for half in range(2):
-                there = 2 * group + half
+            for half, there in enumerate((far, near)):
                 lines[chan, there] = total[:, half * 128 : (half + 1) * 128]
-
-                @pl.when(there != lat)
-                def _():
-                    pltpu.make_async_remote_copy(
-                        src_ref=lines.at[chan, there],
-                        dst_ref=columns.at[chan, lat],
-                        send_sem=line_send.at[chan],
-                        recv_sem=line_recv.at[chan],
-                        device_id=(there, lon),
-                        device_id_type=MESH,
-                    ).start()
+                copy = pltpu.make_async_remote_copy(
+                    src_ref=lines.at[chan, there],
+                    dst_ref=columns.at[chan, lat],
+                    send_sem=line_send.at[chan],
+                    recv_sem=line_recv.at[chan],
+                    device_id=(there, lon),
+                    device_id_type=MESH,
+                )
+                if half == 0:
+                    copy.start()
+                else:
+                    pl.when(step > 0)(copy.start)
 
             return carry
 
-        lax.fori_loop(1, 9, line_group, 0, unroll=2)
+        lax.fori_loop(0, 8, line_group, 0, unroll=2)
 
     def finish(chan):
         wait_for(columns.at[chan, pl.ds(0, LATS - 1)], line_recv.at[chan])
@@ -328,11 +334,11 @@
     wait_for(lat_raw, load_sem.at[1])
     lax.fori_loop(0, 8, prepare_lat, 0)
     lax.fori_loop(0, 8, send_group(1), 0)
-    for group in range(8):
+    for group in range(4):
         add_group(0, group)
     fold(0)
     send_lines(0)
-    for group in range(8):
+    for group in range(4):
         add_group(1, group)
     fold(1)
     send_lines(1)

time: 41.9 us -> 39.5 us (0.943)
  Pallas kernels: 40.9 us -> 38.4 us
    pallas_call x1, Pallas kernels: 40.9 us -> 38.4 us  [on_device(): pl.pallas_call(kernel, out_shape=jax.ShapeDtypeStruct((2, NLAT, 128), F32...]
where the time goes in v4:
time: 39.5 us; the launch traced here: 39.4 us
  Pallas kernels  38.4 us (97%)
  local copies, waits for them, and re-layouts  0.97 us (2%)
    pallas_call x1, Pallas kernels, on_device(): pl.pallas_call(kernel, out_shape=jax.ShapeDtypeStruct((2, NLAT, 128), F32...  38.4 us
    unnamed x1, local copies, waits for them, and re-layouts  0.97 us

profile of v4, /device:TPU:1, one launch (start us, length us, event | category | flops | bytes accessed | tf_op | source)
XLA Modules:
  0.0 39.4 jit_solution(7119121484527036401)
XLA Ops:
  0.0 38.4 %shard_map.73 = f32[2,1024,128]{2,1,0:T(8,128)S(1)} custom-call(bf16[128,16,128]{2,1,0:T(8,128)(2,1)} %cot_hbm.1, f32[128,2,128]{2,1,0:T(2,128)} %frac_hbm.1, s32[128,2,128]{2,1,0:T(2,128)} %off_hbm.1, s32[1,128]{1,0:T(1,128)} %bitcast.2, s32[1,128]{1,0:T(1,128)} %bitcast.3, f32[2048,2048]{1,0:T(8,128)} %lon_ref.1, f32[1024,1024]{1,0:T(8,128)} %lat_ref.1), custom_call_target="tpu_custom_call" | custom-call | tf_op jit(solution)/shard_map/pallas_call | solution.py:360
  38.4 1.0 %copy.9 = f32[2,1024,128]{2,1,0:T(8,128)} copy(f32[2,1024,128]{2,1,0:T(8,128)S(1)} %shard_map.73) | data formatting | bytes 2097152

commit v5 on v4

--- a/solution.py
+++ b/solution.py
@@ -30,11 +30,6 @@
 
 def wait_for(view, sem):
     pltpu.make_async_copy(view, view, sem).wait()
-
-
-def sublane_places(first):
-    row = lax.broadcasted_iota(jnp.int32, (8, 128), 0)
-    return jnp.where(row < 3, row + 8, first(row)).astype(F32)
 
 
 def kernel(cot_hbm, frac_hbm, off_hbm, owner_hbm, sub_hbm, lon_ref, lat_ref, out_ref,
@@ -86,24 +81,27 @@
     index = lax.broadcasted_iota(jnp.int32, (8, 128), 0)
     low = index.astype(F32)
     low_tail = index < 3
-    ends_a = sublane_places(lambda row: row - 3)
-    ends_b = sublane_places(lambda row: row + 2)
-    ends_c = sublane_places(lambda row: jnp.where(row < 6, 10, 15))
-    lat_c = jnp.where(low_tail, 6, jnp.where(index < 6, index + 5, 15)).astype(F32)
+    head_end = index < 6
 
     def window_group(group, carry):
         places = off_ref[pl.ds(group * 8, 8)].astype(F32) + 1.0 + frac_ref[pl.ds(group * 8, 8)]
+        stencils = []
         for item in range(8):
-            block = group * 8 + item
             centre_lat = jnp.broadcast_to(places[item, 0:1, :], (8, 128))
             centre_lon = jnp.broadcast_to(places[item, 1:2, :], (8, 128))
+            lat_tail = spline(low + 8.0 - centre_lat) * (1.0 / 36.0)
             lat_tab[item, 0:8, :] = spline(low - centre_lat) * (1.0 / 36.0)
-            lat_tab[item, 8:16, :] = spline(low + 8.0 - centre_lat) * (1.0 / 36.0)
-            lat_last = spline(lat_c - centre_lat) * (1.0 / 36.0)
+            lat_tab[item, 8:16, :] = lat_tail
             lon_head = spline(low - centre_lon)
-            tail_a = spline(ends_a - centre_lon)
-            tail_b = spline(ends_b - centre_lon)
-            tail_c = spline(ends_c - centre_lon)
+            lon_tail = spline(low + 8.0 - centre_lon)
+            lat_tab[item, 16:24, :] = lon_tail
+            tail_a = jnp.where(low_tail, lon_tail, pltpu.roll(lon_head, 3, 0))
+            tail_b = jnp.where(head_end, pltpu.roll(lon_head, 6, 0), pltpu.roll(lon_tail, 6, 0))
+            tail_b = jnp.where(low_tail, lon_tail, tail_b)
+            tail_c = jnp.where(
+                low_tail, lon_tail, jnp.broadcast_to(lat_tab[item, 18:19, :], (8, 128))
+            )
+            lat_last = pltpu.roll(lat_tail, 3, 0)
 
             def lat_row(w):
                 return jnp.broadcast_to(lat_tab[item, w : w + 1, :], (8, 128))
@@ -115,26 +113,46 @@
                 if w < 6:
                     tail_lat = jnp.where(low_tail, row, high_rows[w % 3])
                 elif w == 6:
-                    tail_lat = lat_last
+                    tail_lat = jnp.where(low_tail, row, lat_last)
                 else:
                     tail_lat = row
                 tail_lon = tail_a if w < 3 else (tail_b if w < 6 else tail_c)
                 pieces.append(row * lon_head)
                 pieces.append(tail_lat * tail_lon)
-            stencil = jnp.concatenate(pieces, axis=0).astype(BF16)
-            window = lax.dot_general(
-                cot_ref[block], stencil, (((1,), (1,)), ((), ())), preferred_element_type=F32
-            )
-            windows[pl.ds(pl.multiple_of(block * CHANS, CHANS), CHANS), :] = window
+            stencils.append(jnp.concatenate(pieces, axis=0).astype(BF16))
+
+        zero = jnp.zeros((CHANS, 128), BF16)
+        for quad in range(2):
+            four = [stencils[4 * quad + item] for item in range(4)]
+            right = jnp.concatenate(
+                [
+                    jnp.concatenate([four[0], four[1]], axis=1),
+                    jnp.concatenate([four[2], four[3]], axis=1),
+                ],
+                axis=0,
+            )
+            rows = []
+            for item in range(4):
+                grads = cot_ref[group * 8 + quad * 4 + item]
+                rows.append(
+                    jnp.concatenate([zero, grads] if item % 2 else [grads, zero], axis=1)
+                )
+            product = lax.dot_general(
+                jnp.concatenate(rows, axis=0), right, (((1,), (1,)), ((), ())),
+                preferred_element_type=F32,
+            )
+            first = pl.multiple_of(group * 128 + quad * 64, 64)
+            windows[pl.ds(first, 32), :] = product[:32, :128]
+            windows[pl.ds(first + 32, 32), :] = product[32:, 128:]
         return carry
 
-    lax.fori_loop(0, 12, window_group, 0)
+    lax.fori_loop(0, 12, window_group, 0, unroll=4)
 
     pl.semaphore_wait(barrier, LATS - 1 + LONS - 1)
 
     for lon_to in lon_there[1:]:
         greet(ready_sem, lat, lon_to)
-    lax.fori_loop(12, 16, window_group, 0)
+    lax.fori_loop(12, 16, window_group, 0, unroll=4)
 
     own_across = jnp.broadcast_to(owner_ref[...].astype(F32), (BLOCKS, BLOCKS))
     own_down = own_across.T
@@ -274,7 +292,7 @@
                 ).astype(BF16)
             return carry
 
-        lax.fori_loop(0, 5, fold_pair, 0)
+        lax.fori_loop(0, 5, fold_pair, 0, unroll=5)
 
     def send_lines(chan):
         def line_group(step, carry):
@@ -320,7 +338,7 @@
                     column_sum[pl.ds(start, 16), :] = value
             return carry
 
-        lax.fori_loop(0, LATS, assemble, 0)
+        lax.fori_loop(0, LATS, assemble, 0, unroll=4)
         column_sum[NLAT : NLAT + 8, :] = columns[chan, LATS - 1, 64:80, :].astype(F32)[0:8]
         whole = column_sum[1 : NLAT + 1, :].astype(BF16)
         for piece in range(4):
@@ -368,7 +386,7 @@
             pltpu.VMEM((BLOCKS, 2, 128), jnp.int32),
             pltpu.VMEM((1, BLOCKS), jnp.int32),
             pltpu.VMEM((1, BLOCKS), jnp.int32),
-            pltpu.VMEM((8, 16, 128), F32),
+            pltpu.VMEM((8, 24, 128), F32),
             pltpu.VMEM((BLOCKS * CHANS, 128), F32),
             pltpu.VMEM((2, LONS, 256, 128), BF16),
             pltpu.VMEM((2, STEPS, PAIR, 128), BF16),

time: 39.5 us -> 38.6 us (0.977)
  Pallas kernels: 38.4 us -> 37.5 us
    pallas_call x1, Pallas kernels: 38.4 us -> 37.5 us  [on_device(): pl.pallas_call(kernel, out_shape=jax.ShapeDtypeStruct((2, NLAT, 128), F32...]
where the time goes in v5:
time: 38.6 us; the launch traced here: 38.5 us
  Pallas kernels  37.5 us (97%)
  local copies, waits for them, and re-layouts  0.97 us (3%)
    pallas_call x1, Pallas kernels, on_device(): pl.pallas_call(kernel, out_shape=jax.ShapeDtypeStruct((2, NLAT, 128), F32...  37.5 us
    unnamed x1, local copies, waits for them, and re-layouts  0.97 us

profile of v5, /device:TPU:1, one launch (start us, length us, event | category | flops | bytes accessed | tf_op | source)
XLA Modules:
  0.0 38.5 jit_solution(9654508601295917262)
XLA Ops:
  0.0 37.5 %shard_map.73 = f32[2,1024,128]{2,1,0:T(8,128)S(1)} custom-call(bf16[128,16,128]{2,1,0:T(8,128)(2,1)} %cot_hbm.1, f32[128,2,128]{2,1,0:T(2,128)} %frac_hbm.1, s32[128,2,128]{2,1,0:T(2,128)} %off_hbm.1, s32[1,128]{1,0:T(1,128)} %bitcast.2, s32[1,128]{1,0:T(1,128)} %bitcast.3, f32[2048,2048]{1,0:T(8,128)} %lon_ref.1, f32[1024,1024]{1,0:T(8,128)} %lat_ref.1), custom_call_target="tpu_custom_call" | custom-call | tf_op jit(solution)/shard_map/pallas_call | solution.py:378
  37.5 1.0 %copy.9 = f32[2,1024,128]{2,1,0:T(8,128)} copy(f32[2,1024,128]{2,1,0:T(8,128)S(1)} %shard_map.73) | data formatting | bytes 2097152

commit v6 on v5

--- a/solution.py
+++ b/solution.py
@@ -146,13 +146,13 @@
             windows[pl.ds(first + 32, 32), :] = product[32:, 128:]
         return carry
 
-    lax.fori_loop(0, 12, window_group, 0, unroll=4)
+    lax.fori_loop(0, 8, window_group, 0, unroll=4)
 
     pl.semaphore_wait(barrier, LATS - 1 + LONS - 1)
 
     for lon_to in lon_there[1:]:
         greet(ready_sem, lat, lon_to)
-    lax.fori_loop(12, 16, window_group, 0, unroll=4)
+    lax.fori_loop(8, 16, window_group, 0, unroll=4)
 
     own_across = jnp.broadcast_to(owner_ref[...].astype(F32), (BLOCKS, BLOCKS))
     own_down = own_across.T
@@ -319,7 +319,7 @@
 
             return carry
 
-        lax.fori_loop(0, 8, line_group, 0, unroll=2)
+        lax.fori_loop(0, 8, line_group, 0, unroll=8)
 
     def finish(chan):
         wait_for(columns.at[chan, pl.ds(0, LATS - 1)], line_recv.at[chan])

time: 38.6 us -> 37.7 us (0.977)
  Pallas kernels: 37.5 us -> 36.6 us
    pallas_call x1, Pallas kernels: 37.5 us -> 36.6 us  [on_device(): pl.pallas_call(kernel, out_shape=jax.ShapeDtypeStruct((2, NLAT, 128), F32...]
where the time goes in v6:
time: 37.7 us; the launch traced here: 37.6 us
  Pallas kernels  36.6 us (97%)
  local copies, waits for them, and re-layouts  0.97 us (3%)
    pallas_call x1, Pallas kernels, on_device(): pl.pallas_call(kernel, out_shape=jax.ShapeDtypeStruct((2, NLAT, 128), F32...  36.6 us
    unnamed x1, local copies, waits for them, and re-layouts  0.97 us

profile of v6, /device:TPU:1, one launch (start us, length us, event | category | flops | bytes accessed | tf_op | source)
XLA Modules:
  0.0 37.6 jit_solution(7928047161318684980)
XLA Ops:
  0.0 36.6 %shard_map.73 = f32[2,1024,128]{2,1,0:T(8,128)S(1)} custom-call(bf16[128,16,128]{2,1,0:T(8,128)(2,1)} %cot_hbm.1, f32[128,2,128]{2,1,0:T(2,128)} %frac_hbm.1, s32[128,2,128]{2,1,0:T(2,128)} %off_hbm.1, s32[1,128]{1,0:T(1,128)} %bitcast.2, s32[1,128]{1,0:T(1,128)} %bitcast.3, f32[2048,2048]{1,0:T(8,128)} %lon_ref.1, f32[1024,1024]{1,0:T(8,128)} %lat_ref.1), custom_call_target="tpu_custom_call" | custom-call | tf_op jit(solution)/shard_map/pallas_call | solution.py:378
  36.6 1.0 %copy.9 = f32[2,1024,128]{2,1,0:T(8,128)} copy(f32[2,1024,128]{2,1,0:T(8,128)S(1)} %shard_map.73) | data formatting | bytes 2097152
